TPU v7x, 32 devices: a whole 2x2x4 slice. The times are simulated.
32 devices in a mesh: dp: 4 (over y, x), ctx: 2 (over core), tp: 4 (over z).
Axes of the slice: x: 2, y: 2, z: 4, core: 2. Of those that a mesh axis runs over, the one named last changes fastest.
Arguments:
- block_input: bfloat16 [2048, 1024], P(('dp', 'ctx')), may hold values from -6 to 6
- qkv_weight: bfloat16 [1024, 3, 1024], P('dp', None, 'tp'), may hold values from -0.125 to 0.125
- qv_bias: bfloat16 [2, 16, 64], P(None, 'tp', 'dp'), may hold values from -3 to 3
- proj_weight: bfloat16 [1024, 1024], P('dp', 'tp'), may hold values from -0.75 to 0.75
- fc_weight: bfloat16 [1024, 4096], P('dp', 'tp'), may hold values from -0.1875 to 0.1875
- fc_bias: bfloat16 [32, 128], P('tp', 'dp'), may hold values from -3 to 3
- out_weight: bfloat16 [1024, 4096], P('dp', 'tp'), may hold values from -0.09375 to 0.09375
- norm_gains: bfloat16 [2, 1024], P(None, 'dp'), may hold values from 0.5 to 1.5
- shifts: bfloat16 [4, 1024], P(None, 'dp'), may hold values from -2 to 2
- segment_ids: int32 [4, 512], P('dp'), may hold values from 0 to 3, as said below
- out_grad: bfloat16 [2048, 1024], P(('dp', 'ctx')), may hold values from -6 to 6
Outputs:
- block_output: float32 [2048, 1024], P(('dp', 'ctx'))
- input_grad: float32 [2048, 1024], P(('dp', 'ctx'))
- qkv_weight_grad: float32 [1024, 3, 1024], P('dp', None, 'tp')
- qv_bias_grad: float32 [2, 16, 64], P(None, 'tp', 'dp')
- proj_weight_grad: float32 [1024, 1024], P('dp', 'tp')
- fc_weight_grad: float32 [1024, 4096], P('dp', 'tp')
- fc_bias_grad: float32 [32, 128], P('tp', 'dp')
- out_weight_grad: float32 [1024, 4096], P('dp', 'tp')
- norm_gains_grad: float32 [2, 1024], P(None, 'dp')
- shifts_grad: float32 [4, 1024], P(None, 'dp')
Inputs may be any that keep to these rules, and one draw needn't show every extreme that they name: `segment_ids`: within each sequence the document numbers never fall and all 4 appear; each document covers 64 to 256 positions, one exactly 256 and one exactly 64.
All inputs are finite; a program needn't handle non-finite values.
Results may differ from a plain program's by a relative error of at most 0.012.
Values may be sent and summed in bfloat16 or wider, within the bound.
A program may use at most 128 MiB of HBM per device.

v0:
```python
import jax
import jax.numpy as jnp
from jax import lax
from jax.sharding import PartitionSpec as P

EPSILON = 1e-05
MASKED_SCORE = -1e30
GELU_SCALE = 0.7978845608028654


def layer_norm(values, gain_row, shift_row):
    centered = values - jnp.mean(values, axis=-1, keepdims=True)
    inverse = lax.rsqrt(jnp.mean(centered * centered, axis=-1, keepdims=True) + EPSILON)
    normed = centered * inverse
    return (normed, inverse, normed * gain_row + shift_row)


def norm_back(upstream, normed, inverse, gain_row):
    scaled = upstream * gain_row
    return inverse * (
        scaled
        - jnp.mean(scaled, axis=-1, keepdims=True)
        - normed * jnp.mean(scaled * normed, axis=-1, keepdims=True)
    )


def gelu_slope(pre_act):
    inner_arg = GELU_SCALE * (pre_act + 0.044715 * pre_act * pre_act * pre_act)
    tanh_val = jnp.tanh(inner_arg)
    activated = 0.5 * pre_act * (1.0 + tanh_val)
    slopes = 0.5 * (1.0 + tanh_val) + 0.5 * pre_act * (1.0 - tanh_val * tanh_val) * GELU_SCALE * (
        1.0 + 3.0 * 0.044715 * pre_act * pre_act
    )
    return (activated, slopes)


def blocks_of(array_in, block_count):
    return array_in.reshape((block_count, array_in.shape[0] // block_count) + array_in.shape[1:])


def per_device(
    block_input,
    qkv_weight,
    qv_bias,
    proj_weight,
    fc_weight,
    fc_bias,
    out_weight,
    norm_gains,
    shifts,
    segment_ids,
    out_grad,
):
    tok_rows = block_input.shape[0]
    gathered = (
        lax.all_gather(qkv_weight, "dp", axis=0, tiled=True),
        lax.all_gather(proj_weight, "dp", axis=0, tiled=True),
        lax.all_gather(fc_weight, "dp", axis=0, tiled=True),
        lax.all_gather(out_weight, "dp", axis=0, tiled=True),
        lax.all_gather(qv_bias, "dp", axis=2, tiled=True),
        lax.all_gather(fc_bias, "dp", axis=1, tiled=True),
        lax.all_gather(norm_gains, "dp", axis=1, tiled=True),
        lax.all_gather(shifts, "dp", axis=1, tiled=True),
    )
    w_qkv, w_proj, w_fc, w_out, bias_qv, bias_fc, gains_b, shifts_b = gathered
    gains_f = gains_b.astype(jnp.float32)
    shifts_f = shifts_b.astype(jnp.float32)
    heads_here = bias_qv.shape[1]
    head_dim = bias_qv.shape[2]
    local_width = heads_here * head_dim
    table_shape = bias_fc.shape
    bias_qv_f = bias_qv.astype(jnp.float32).reshape(2, local_width)
    bias_fc_f = bias_fc.astype(jnp.float32).reshape(-1)
    score_scale = head_dim ** (-0.5)
    seq_len = segment_ids.shape[1]
    ctx_index = lax.axis_index("ctx")
    seg_whole = segment_ids[0]
    first_row = ctx_index * tok_rows
    seg_here = lax.dynamic_slice_in_dim(seg_whole, first_row, tok_rows)
    pos_here = first_row + jnp.arange(tok_rows, dtype=jnp.int32)
    key_pos = jnp.arange(seq_len, dtype=jnp.int32)
    block_rows = min(512, tok_rows)
    block_count = tok_rows // block_rows
    input_f32 = block_input.astype(jnp.float32)
    normed1, inverse1, ln1_float = layer_norm(input_f32, gains_f[0], shifts_f[0])
    ln1_out = ln1_float.astype(jnp.bfloat16)
    packed = jnp.einsum("rd,dtc->trc", ln1_out, w_qkv, preferred_element_type=jnp.float32)
    queries = (packed[0] + bias_qv_f[0]).astype(jnp.bfloat16)
    keys_here = packed[1].astype(jnp.bfloat16)
    values_here = (packed[2] + bias_qv_f[1]).astype(jnp.bfloat16)
    keys_all, values_all = (
        lax.all_gather(keys_here, "ctx", axis=0, tiled=True),
        lax.all_gather(values_here, "ctx", axis=0, tiled=True),
    )
    key_heads = keys_all.reshape(seq_len, heads_here, head_dim)
    value_heads = values_all.reshape(seq_len, heads_here, head_dim)

    def scores_of(query_blk, seg_blk, pos_blk):
        raw_scores = (
            jnp.einsum(
                "qhd,khd->hqk",
                query_blk.reshape(-1, heads_here, head_dim),
                key_heads,
                preferred_element_type=jnp.float32,
            )
            * score_scale
        )
        live_mask = (seg_blk[:, None] == seg_whole[None, :]) & (
            key_pos[None, :] <= pos_blk[:, None]
        )
        return jnp.where(live_mask[None], raw_scores, MASKED_SCORE)

    def forward_block(pieces):
        query_blk, seg_blk, pos_blk = pieces
        scores = scores_of(query_blk, seg_blk, pos_blk)
        row_max = jnp.max(scores, axis=-1, keepdims=True)
        log_total = row_max + jnp.log(jnp.sum(jnp.exp(scores - row_max), axis=-1, keepdims=True))
        attn_probs = jnp.exp(scores - log_total).astype(jnp.bfloat16)
        mixed = jnp.einsum(
            "hqk,khd->qhd", attn_probs, value_heads, preferred_element_type=jnp.float32
        )
        return (mixed.reshape(-1, local_width).astype(jnp.bfloat16), log_total)

    attn_blocks, log_totals = lax.map(
        forward_block,
        (
            blocks_of(queries, block_count),
            blocks_of(seg_here, block_count),
            blocks_of(pos_here, block_count),
        ),
    )
    attn_out = attn_blocks.reshape(tok_rows, local_width)
    head_terms = jnp.einsum("rc,dc->rd", attn_out, w_proj, preferred_element_type=jnp.float32)
    resid = input_f32 + lax.psum(head_terms, "tp") + shifts_f[2]
    normed2, inverse2, ln2_float = layer_norm(resid, gains_f[1], shifts_f[1])
    ln2_out = ln2_float.astype(jnp.bfloat16)
    pre_act = jnp.dot(ln2_out, w_fc, preferred_element_type=jnp.float32) + bias_fc_f
    activated, slopes = gelu_slope(pre_act)
    act_b = activated.astype(jnp.bfloat16)
    mlp_terms = jnp.einsum("rf,df->rd", act_b, w_out, preferred_element_type=jnp.float32)
    output = resid + lax.psum(mlp_terms, "tp") + shifts_f[3]
    w_qkv, w_proj, w_fc, w_out, gains_again = (
        lax.all_gather(qkv_weight, "dp", axis=0, tiled=True),
        lax.all_gather(proj_weight, "dp", axis=0, tiled=True),
        lax.all_gather(fc_weight, "dp", axis=0, tiled=True),
        lax.all_gather(out_weight, "dp", axis=0, tiled=True),
        lax.all_gather(norm_gains, "dp", axis=1, tiled=True),
    )
    gains_f = gains_again.astype(jnp.float32)
    grad_f32 = out_grad.astype(jnp.float32)
    out_w_grad = jnp.einsum("rd,rf->df", out_grad, act_b, preferred_element_type=jnp.float32)
    hidden_grad = (jnp.dot(out_grad, w_out, preferred_element_type=jnp.float32) * slopes).astype(
        jnp.bfloat16
    )
    fc_w_grad = jnp.einsum("rd,rf->df", ln2_out, hidden_grad, preferred_element_type=jnp.float32)
    fc_b_grad = jnp.sum(hidden_grad.astype(jnp.float32), axis=0).reshape(table_shape)
    norm2_grad = lax.psum(
        jnp.einsum("rf,df->rd", hidden_grad, w_fc, preferred_element_type=jnp.float32), "tp"
    )
    resid_grad = grad_f32 + norm_back(norm2_grad, normed2, inverse2, gains_f[1])
    resid_grad_b = resid_grad.astype(jnp.bfloat16)
    proj_w_grad = jnp.einsum(
        "rd,rc->dc", resid_grad_b, attn_out, preferred_element_type=jnp.float32
    )
    attn_grad = jnp.dot(resid_grad_b, w_proj, preferred_element_type=jnp.float32).astype(
        jnp.bfloat16
    )

    def backward_block(carry, pieces):
        key_acc, value_acc = carry
        query_blk, seg_blk, pos_blk, log_total, out_blk, grad_blk = pieces
        scores = scores_of(query_blk, seg_blk, pos_blk)
        probs_f = jnp.exp(scores - log_total)
        grad_heads = grad_blk.reshape(-1, heads_here, head_dim)
        query_heads = query_blk.reshape(-1, heads_here, head_dim)
        prob_grad = jnp.einsum(
            "qhd,khd->hqk", grad_heads, value_heads, preferred_element_type=jnp.float32
        )
        row_delta = jnp.sum(
            grad_heads.astype(jnp.float32)
            * out_blk.reshape(-1, heads_here, head_dim).astype(jnp.float32),
            axis=-1,
        )
        score_grad = (
            probs_f * (prob_grad - jnp.transpose(row_delta)[:, :, None]) * score_scale
        ).astype(jnp.bfloat16)
        query_grad = jnp.einsum(
            "hqk,khd->qhd", score_grad, key_heads, preferred_element_type=jnp.float32
        )
        key_acc = key_acc + jnp.einsum(
            "hqk,qhd->khd", score_grad, query_heads, preferred_element_type=jnp.float32
        )
        value_acc = value_acc + jnp.einsum(
            "hqk,qhd->khd",
            probs_f.astype(jnp.bfloat16),
            grad_heads,
            preferred_element_type=jnp.float32,
        )
        return ((key_acc, value_acc), query_grad.reshape(-1, local_width).astype(jnp.bfloat16))

    zero_keys = jnp.zeros((seq_len, heads_here, head_dim), jnp.float32)
    (key_acc, value_acc), query_blocks = lax.scan(
        backward_block,
        (zero_keys, zero_keys),
        (
            blocks_of(queries, block_count),
            blocks_of(seg_here, block_count),
            blocks_of(pos_here, block_count),
            log_totals,
            attn_blocks,
            blocks_of(attn_grad, block_count),
        ),
    )
    query_grad = query_blocks.reshape(tok_rows, local_width)
    key_sum, value_sum = (
        lax.psum_scatter(
            key_acc.reshape(seq_len, local_width), "ctx", scatter_dimension=0, tiled=True
        ),
        lax.psum_scatter(
            value_acc.reshape(seq_len, local_width), "ctx", scatter_dimension=0, tiled=True
        ),
    )
    key_grad = key_sum.astype(jnp.bfloat16)
    value_grad = value_sum.astype(jnp.bfloat16)
    stacked = jnp.stack([query_grad, key_grad, value_grad])
    qkv_w_grad = jnp.einsum("rd,trc->dtc", ln1_out, stacked, preferred_element_type=jnp.float32)
    qv_b_grad = jnp.stack(
        [
            jnp.sum(query_grad.astype(jnp.float32), axis=0),
            jnp.sum(value_grad.astype(jnp.float32), axis=0),
        ]
    ).reshape(2, heads_here, head_dim)
    norm1_grad = lax.psum(
        jnp.einsum("trc,dtc->rd", stacked, w_qkv, preferred_element_type=jnp.float32), "tp"
    )
    input_grad = resid_grad + norm_back(norm1_grad, normed1, inverse1, gains_f[0])
    gains_grad = jnp.stack(
        [jnp.sum(norm1_grad * normed1, axis=0), jnp.sum(norm2_grad * normed2, axis=0)]
    )
    shifts_grad = jnp.stack(
        [
            jnp.sum(norm1_grad, axis=0),
            jnp.sum(norm2_grad, axis=0),
            jnp.sum(resid_grad, axis=0),
            jnp.sum(grad_f32, axis=0),
        ]
    )
    grad_terms = (
        qkv_w_grad,
        proj_w_grad,
        fc_w_grad,
        out_w_grad,
        qv_b_grad,
        fc_b_grad,
        gains_grad,
        shifts_grad,
    )
    owned = (
        lax.psum_scatter(grad_terms[0], "dp", scatter_dimension=0, tiled=True),
        lax.psum_scatter(grad_terms[1], "dp", scatter_dimension=0, tiled=True),
        lax.psum_scatter(grad_terms[2], "dp", scatter_dimension=0, tiled=True),
        lax.psum_scatter(grad_terms[3], "dp", scatter_dimension=0, tiled=True),
        lax.psum_scatter(grad_terms[4], "dp", scatter_dimension=2, tiled=True),
        lax.psum_scatter(grad_terms[5], "dp", scatter_dimension=1, tiled=True),
        lax.psum_scatter(grad_terms[6], "dp", scatter_dimension=1, tiled=True),
        lax.psum_scatter(grad_terms[7], "dp", scatter_dimension=1, tiled=True),
    )
    summed = lax.psum(
        (owned[0], owned[1], owned[2], owned[3], owned[4], owned[5], owned[6], owned[7]), "ctx"
    )
    g_qkv, g_proj, g_fc, g_out, g_qv, g_fc_bias, g_gains, g_shifts = summed
    return (output, input_grad, g_qkv, g_qv, g_proj, g_fc, g_fc_bias, g_out, g_gains, g_shifts)


def solution(mesh):
    in_specs = (
        P(("dp", "ctx"), None),
        P("dp", None, "tp"),
        P(None, "tp", "dp"),
        P("dp", "tp"),
        P("dp", "tp"),
        P("tp", "dp"),
        P("dp", "tp"),
        P(None, "dp"),
        P(None, "dp"),
        P("dp", None),
        P(("dp", "ctx"), None),
    )
    out_specs = (
        P(("dp", "ctx"), None),
        P(("dp", "ctx"), None),
        P("dp", None, "tp"),
        P(None, "tp", "dp"),
        P("dp", "tp"),
        P("dp", "tp"),
        P("tp", "dp"),
        P("dp", "tp"),
        P(None, "dp"),
        P(None, "dp"),
    )
    return jax.shard_map(
        per_device, mesh=mesh, in_specs=in_specs, out_specs=out_specs, check_vma=False
    )
```

profile of v0, /device:TPU:0, one launch (start us, length us, event | category | flops | bytes accessed | tf_op | source)
XLA Modules:
  0.0 674.2 jit_solution(12836303677747407799)
XLA Ops:
  7.2 2.0 copy.46
  9.3 0.8 copy.47
  10.1 9.6 %all_gather.38 = bf16[2,4,64]{1,0,2:T(2,128)(2,1)S(1)} all-gather(bf16[2,4,16]{1,0,2:T(2,128)(2,1)S(1)} %copy.47), channel_id=1, replica_groups=mesh['dp'=4,'ctx'=2,'tp'=4] {'dp'}, dimensions={2}, use_global_device_ids=true | all-gather | bytes 1280 | tf_op jit(solution)/shard_map/all_gather | solution.py:60
  20.0 8.1 %all_gather.35 = bf16[2,1024]{1,0:T(2,128)(2,1)S(1)} all-gather(bf16[2,256]{1,0:T(2,128)(2,1)} %param.18), channel_id=1, replica_groups=mesh['dp'=4,'ctx'=2,'tp'=4] {'dp'}, dimensions={1}, use_global_device_ids=true | all-gather | bytes 5120 | tf_op jit(solution)/shard_map/all_gather | solution.py:62
  28.0 7.2 %all_gather.36 = bf16[4,1024]{1,0:T(4,128)(2,1)S(1)} all-gather(bf16[4,256]{1,0:T(4,128)(2,1)} %param.19), channel_id=1, replica_groups=mesh['dp'=4,'ctx'=2,'tp'=4] {'dp'}, dimensions={1}, use_global_device_ids=true | all-gather | bytes 10240 | tf_op jit(solution)/shard_map/all_gather | solution.py:63
  35.2 12.0 %all_gather.41 = bf16[1024,256]{1,0:T(8,128)(2,1)S(1)} all-gather(bf16[256,256]{1,0:T(8,128)(2,1)} %param.14), channel_id=1, replica_groups=mesh['dp'=4,'ctx'=2,'tp'=4] {'dp'}, dimensions={0}, use_global_device_ids=true | all-gather | bytes 655360 | tf_op jit(solution)/shard_map/all_gather | solution.py:57
  48.6 2.1 convolution_bitcast_fusion.2
  50.8 2.0 all-gather
  52.8 0.7 copy-done.11
  53.5 0.8 fusion.46
  55.1 2.0 all_gather.39
  57.7 1.3 fusion.47
  60.4 8.0 %all-gather.1 = bf16[4,32,8]{1,2,0:T(8,128)(2,1)S(1)} all-gather(bf16[1,32,8]{1,2,0:T(8,128)(2,1)S(1)} %bitcast.142), channel_id=1, replica_groups=mesh['dp'=4,'ctx'=2,'tp'=4] {'dp'}, dimensions={0}, use_global_device_ids=true | all-gather | bytes 2560 | tf_op jit(solution)/shard_map/all_gather | solution.py:61
  69.1 41.9 %all-reduce.9.cloned.1.call-done = f32[256,1024]{1,0:T(8,128)} async-done(((f32[256,1024]{1,0:T(8,128)}), f32[256,1024]{1,0:T(8,128)}) %all-reduce.9.cloned.1.call-update) | async-done | bytes 1048592 | tf_op jit(solution)/shard_map/psum | solution.py:134
  111.0 1.6 fusion.41
  114.1 33.7 %all-gather.8.cloned.1.call-done = bf16[1024,1024]{1,0:T(8,128)(2,1)} async-done(((bf16[256,1024]{1,0:T(8,128)(2,1)}), bf16[1024,1024]{1,0:T(8,128)(2,1)}) %all-gather.8.cloned.1.call-update) | async-done | bytes 2097168 | tf_op jit(solution)/shard_map/all_gather | solution.py:58
  147.8 3.3 convolution_add_fusion
  151.1 33.9 %all-gather.10.cloned.1.call-done = bf16[1024,1024]{1,0:T(8,128)(2,1)} async-done(((bf16[256,1024]{1,0:T(8,128)(2,1)}), bf16[1024,1024]{1,0:T(8,128)(2,1)}) %all-gather.10.cloned.1.call-update) | async-done | bytes 2097168 | tf_op jit(solution)/shard_map/all_gather | solution.py:59
  185.0 3.9 convert_reduce_fusion.2
  188.9 0.8 copy-done.17
  189.7 1.7 fusion.48
  191.5 51.9 %all-reduce.11.cloned.1.call-done = f32[256,1024]{1,0:T(8,128)} async-done(((f32[256,1024]{1,0:T(8,128)}), f32[256,1024]{1,0:T(8,128)}) %all-reduce.11.cloned.1.call-update) | async-done | bytes 1048592 | tf_op jit(solution)/shard_map/psum | solution.py:157
  243.4 2.4 multiply_reduce_fusion
  245.9 1.9 fusion.40
  249.1 1.1 fusion.35
  250.3 2.0 copy.51
  252.4 2.2 fusion.24
  254.6 2.0 copy.52
  256.9 4.0 fusion.38
  260.9 1.1 convert_reduce_fusion.4
  262.2 1.0 convert_bitcast_fusion
  263.2 8.1 %reduce-scatter.19.cloned.1.call-done = f32[256,256]{1,0:T(8,128)} async-done(((f32[512,256]{1,0:T(8,128)}), f32[256,256]{1,0:T(8,128)}) %reduce-scatter.19.cloned.1.call-update) | async-done | bytes 262160 | tf_op jit(solution)/shard_map/reduce_scatter | solution.py:219
  271.3 1.5 convert_reduce_fusion.3
  272.9 3.0 convolution_bitcast_fusion.1
  276.0 1.3 fusion.29
  277.5 2.8 fusion.39
  280.3 1.1 copy-done.10
  281.5 3.9 convolution_bitcast_fusion
  285.5 1.0 copy-done.1
  286.5 2.5 fusion.32
  289.7 0.7 copy.62
  290.5 73.8 %all-reduce.13.cloned.1.call-done = (f32[256,1024]{1,0:T(8,128)}, f32[256,1024]{1,0:T(8,128)}) async-done(((f32[256,1024]{1,0:T(8,128)}, f32[256,1024]{1,0:T(8,128)}), (f32[256,1024]{1,0:T(8,128)}, f32[256,1024]{1,0:T(8,128)})) %all-reduce.13.cloned.1.call-update) | async-done | bytes 2097168 | tf_op jit(solution)/shard_map/psum | solution.py:141
  364.3 1.8 fusion.14
  366.1 1.0 copy.64
  367.3 1.0 copy.66
  368.4 26.4 %reduce-scatter.23.cloned.1.call-done = f32[256,256]{1,0:T(8,128)} async-done(((f32[1024,256]{1,0:T(8,128)}), f32[256,256]{1,0:T(8,128)}) %reduce-scatter.23.cloned.1.call-update) | async-done | bytes 262160 | tf_op jit(solution)/shard_map/reduce_scatter | solution.py:260
  394.7 55.6 %reduce-scatter.25.cloned.1.call-done = f32[256,1024]{1,0:T(8,128)} async-done(((f32[1024,1024]{1,0:T(8,128)}), f32[256,1024]{1,0:T(8,128)}) %reduce-scatter.25.cloned.1.call-update) | async-done | bytes 1048592 | tf_op jit(solution)/shard_map/reduce_scatter | solution.py:261
  450.3 55.9 %reduce-scatter.27.cloned.1.call-done = f32[256,1024]{0,1:T(8,128)} async-done(((f32[1024,1024]{0,1:T(8,128)}), f32[256,1024]{0,1:T(8,128)}) %reduce-scatter.27.cloned.1.call-update) | async-done | bytes 1048592 | tf_op jit(solution)/shard_map/reduce_scatter | solution.py:262
  506.2 46.8 %reduce-scatter.21.cloned.1.call-done = f32[256,3,256]{2,0,1:T(8,128)} async-done(((f32[1024,3,256]{2,0,1:T(8,128)}), f32[256,3,256]{2,0,1:T(8,128)}) %reduce-scatter.21.cloned.1.call-update) | async-done | bytes 786448 | tf_op jit(solution)/shard_map/reduce_scatter | solution.py:259
  554.3 25.7 %reduce-scatter.29.cloned.1.call-done = f32[32,8]{1,0:T(8,128)} async-done(((f32[128,8]{1,0:T(8,128)}), f32[32,8]{1,0:T(8,128)}) %reduce-scatter.29.cloned.1.call-update) | async-done | bytes 1040
  580.0 0.8 copy.63
  580.9 8.9 %all-reduce = f32[2,4,64]{2,1,0:T(4,128)S(1)} all-reduce(f32[2,4,64]{2,1,0:T(4,128)S(1)} %pad_maximum_fusion.5), channel_id=6, replica_groups=mesh['dp'=4,'ctx'=2,'tp'=4] {'dp'}, use_global_device_ids=true, to_apply=%region_21.22.clone | all-reduce | flops 512 | bytes 4096
  589.9 2.4 add_add_fusion
  592.4 1.4 fusion.13
  593.7 14.6 %reduce-scatter.31.cloned.1.call-done = f32[256,2]{1,0:T(8,128)} async-done(((f32[1024,2]{1,0:T(8,128)}), f32[256,2]{1,0:T(8,128)}) %reduce-scatter.31.cloned.1.call-update) | async-done | bytes 2064
  608.4 1.0 copy.65
  609.3 27.1 %reduce-scatter.33.cloned.1.call-done = f32[256,4]{1,0:T(8,128)} async-done(((f32[1024,4]{1,0:T(8,128)}), f32[256,4]{1,0:T(8,128)}) %reduce-scatter.33.cloned.1.call-update) | async-done | bytes 4112
  636.4 1.0 copy.67
  637.4 3.9 all-reduce.2
  641.3 21.1 %all-reduce.15.cloned.1.call-done = (f32[256,3,256]{2,0,1:T(8,128)}, f32[256,256]{1,0:T(8,128)}, f32[256,1024]{1,0:T(8,128)}, f32[256,1024]{0,1:T(8,128)}) async-done(((f32[256,3,256]{2,0,1:T(8,128)}, f32[256,256]{1,0:T(8,128)}, f32[256,1024]{1,0:T(8,128)}, f32[256,1024]{0,1:T(8,128)}), (f32[256,3,256]{2,0,1:T(8,128)}, f32[256,256]{1,0:T(8,128)}, f32[256,1024]{1,0:T(8,128)}, ...) | async-done | bytes 3145744 | tf_op jit(solution)/shard_map/psum | solution.py:268
  662.4 2.7 copy.56
  665.1 0.9 copy.76
  666.0 0.7 copy.77
  666.7 1.0 copy.78
  (158 shorter events, 10.3 us)
Async XLA Ops:
  7.2 40.1 %copy-start.41 = (s32[1,512]{1,0:T(1,128)S(1)}, s32[1,512]{1,0:T(1,128)}, u32[]{:S(2)}) copy-start(s32[1,512]{1,0:T(1,128)} %param.20) | copy-start | bytes 6148
  7.2 40.1 %copy-start = (bf16[256,1024]{1,0:T(8,128)(2,1)S(1)}, bf16[256,1024]{1,0:T(8,128)(2,1)}, u32[]{:S(2)}) copy-start(bf16[256,1024]{1,0:T(8,128)(2,1)} %param.11) | copy-start | bytes 1572868
  7.2 41.4 %all-gather.6.cloned.1.call-start = ((), (), s32[]{:S(2)}) async-start(), calls=%async_computation.9 | async-start | bytes 1966080 | tf_op jit(solution)/shard_map/all_gather | solution.py:56
  9.2 101.8 %all-reduce.9.cloned.1.call-start = ((), (), s32[]{:S(2)}) async-start(), calls=%async_computation.10 | async-start | bytes 2097152 | tf_op jit(solution)/shard_map/psum | solution.py:134
  19.8 33.0 %copy-start.27 = (f32[4,64]{1,0:T(4,128)}, f32[4,64]{1,0:T(4,128)S(1)}, u32[]{:S(2)}) copy-start(f32[4,64]{1,0:T(4,128)S(1)} %copy.49) | copy-start | bytes 3076
  47.3 10.4 %copy-start.6 = (bf16[1024,256]{1,0:T(8,128)(2,1)}, bf16[1024,256]{1,0:T(8,128)(2,1)S(1)}, u32[]{:S(2)}) copy-start(bf16[1024,256]{1,0:T(8,128)(2,1)S(1)} %all_gather.41) | copy-start | bytes 1572868
  47.8 3.1 copy-start.29
  48.4 2.4 copy-start.33
  50.8 3.5 copy-start.13
  52.8 0.7 copy-start.11
  57.7 2.7 copy-start.44
  59.0 88.7 %all-gather.8.cloned.1.call-start = ((), (), s32[]{:S(2)}) async-start(), calls=%async_computation.11 | async-start | bytes 2621440 | tf_op jit(solution)/shard_map/all_gather | solution.py:58
  59.8 125.2 %all-gather.10.cloned.1.call-start = ((), (), s32[]{:S(2)}) async-start(), calls=%async_computation.12 | async-start | bytes 2621440 | tf_op jit(solution)/shard_map/all_gather | solution.py:59
  60.3 183.1 %all-reduce.11.cloned.1.call-start = ((), (), s32[]{:S(2)}) async-start(), calls=%async_computation.13 | async-start | bytes 2097152 | tf_op jit(solution)/shard_map/psum | solution.py:157
  112.6 0.6 copy-start.25
  185.0 4.7 copy-start.16
  188.9 0.8 copy-start.17
  191.4 70.8 %reduce-scatter.17.cloned.1.call-start = ((), (), s32[]{:S(2)}) async-start(), calls=%async_computation.14 | async-start | bytes 786432 | tf_op jit(solution)/shard_map/reduce_scatter | solution.py:216
  243.4 2.5 copy-start.9
  243.4 2.5 copy-start.15
  245.9 1.9 copy-start.7
  247.7 1.1 copy-start.2
  248.1 2.2 copy-start.19
  248.1 1.0 copy-start.14
  248.1 1.0 copy-start.28
  249.1 1.1 copy-start.4
  252.3 19.0 %reduce-scatter.19.cloned.1.call-start = ((), (), s32[]{:S(2)}) async-start(), calls=%async_computation.15 | async-start | bytes 786432 | tf_op jit(solution)/shard_map/reduce_scatter | solution.py:219
  256.7 4.3 copy-start.5
  256.7 4.3 copy-start.12
  256.7 107.6 %all-reduce.13.cloned.1.call-start = ((), (), s32[]{:S(2)}) async-start(), calls=%async_computation.23 | async-start | bytes 4194304 | tf_op jit(solution)/shard_map/psum | solution.py:141
  262.2 13.7 %copy-start.20 = (bf16[1,256,256]{2,1,0:T(8,128)(2,1)}, bf16[1,256,256]{2,1,0:T(8,128)(2,1)S(1)}, u32[]{:S(2)}) copy-start(bf16[1,256,256]{2,1,0:T(8,128)(2,1)S(1)} %copy.53) | copy-start | bytes 393220
  272.8 3.2 copy-start.3
  275.9 1.5 copy-start.18
  275.9 1.5 copy-start.26
  275.9 1.5 copy-start.38
  276.0 1.5 copy-start.39
  276.0 118.8 %reduce-scatter.23.cloned.1.call-start = ((), (), s32[]{:S(2)}) async-start(), calls=%async_computation.17 | async-start | bytes 1310720 | tf_op jit(solution)/shard_map/reduce_scatter | solution.py:260
  277.4 172.9 %reduce-scatter.25.cloned.1.call-start = ((), (), s32[]{:S(2)}) async-start(), calls=%async_computation.18 | async-start | bytes 5242880 | tf_op jit(solution)/shard_map/reduce_scatter | solution.py:261
  280.3 1.2 copy-start.10
  280.3 225.9 %reduce-scatter.27.cloned.1.call-start = ((), (), s32[]{:S(2)}) async-start(), calls=%async_computation.19 | async-start | bytes 5242880 | tf_op jit(solution)/shard_map/reduce_scatter | solution.py:262
  285.4 1.0 copy-start.1
  285.4 1.1 copy-start.21
  285.4 1.1 copy-start.30
  285.5 1.1 copy-start.34
  285.5 267.5 %reduce-scatter.21.cloned.1.call-start = ((), (), s32[]{:S(2)}) async-start(), calls=%async_computation.16 | async-start | bytes 3932160 | tf_op jit(solution)/shard_map/reduce_scatter | solution.py:259
  289.0 0.7 copy-start.43
  289.0 77.0 %copy-start.31 = (f32[1024]{0:T(1024)S(1)}, f32[1024]{0:T(1024)}, u32[]{:S(2)}) copy-start(f32[1024]{0:T(1024)} %get-tuple-element.122) | copy-start | bytes 12292
  289.0 78.1 %copy-start.35 = (f32[1024]{0:T(1024)S(1)}, f32[1024]{0:T(1024)}, u32[]{:S(2)}) copy-start(f32[1024]{0:T(1024)} %get-tuple-element.129) | copy-start | bytes 12292
  289.0 78.1 %copy-start.36 = (f32[1024]{0:T(1024)S(1)}, f32[1024]{0:T(1024)}, u32[]{:S(2)}) copy-start(f32[1024]{0:T(1024)} %get-tuple-element.140) | copy-start | bytes 12292
  289.1 78.1 %copy-start.37 = (f32[1024]{0:T(1024)S(1)}, f32[1024]{0:T(1024)}, u32[]{:S(2)}) copy-start(f32[1024]{0:T(1024)} %get-tuple-element.144) | copy-start | bytes 12292
  289.1 290.9 %reduce-scatter.29.cloned.1.call-start = ((), (), s32[]{:S(2)}) async-start(), calls=%async_computation.20 | async-start | bytes 81920
  290.5 317.9 %reduce-scatter.31.cloned.1.call-start = ((), (), s32[]{:S(2)}) async-start(), calls=%async_computation.21 | async-start | bytes 655360
  367.1 269.3 %reduce-scatter.33.cloned.1.call-start = ((), (), s32[]{:S(2)}) async-start(), calls=%async_computation.22 | async-start | bytes 655360
  367.2 185.8 %copy-start.45 = (u32[32]{0:T(128)S(1)}, u32[32]{0:T(128)}, u32[]{:S(2)}) copy-start(u32[32]{0:T(128)} %constant.85) | copy-start | bytes 388
  367.2 213.5 %copy-start.42 = (f32[256]{0:T(256)S(1)}, f32[256]{0:T(256)}, u32[]{:S(2)}) copy-start(f32[256]{0:T(256)} %get-tuple-element.145) | copy-start | bytes 3076
  367.3 213.6 %copy-start.40 = (f32[4,64]{1,0:T(4,128)S(1)}, f32[4,64]{1,0:T(4,128)}, u32[]{:S(2)}) copy-start(f32[4,64]{1,0:T(4,128)} %get-tuple-element.159) | copy-start | bytes 3076
  367.3 222.6 %copy-start.32 = (f32[1,1024]{1,0:T(1,128)S(1)}, f32[1,1024]{1,0:T(1,128)}, u32[]{:S(2)}) copy-start(f32[1,1024]{1,0:T(1,128)} %get-tuple-element.149) | copy-start | bytes 12292
  368.3 294.1 %all-reduce.15.cloned.1.call-start = ((), (), s32[]{:S(2)}) async-start(), calls=%async_computation.24 | async-start | bytes 6291456 | tf_op jit(solution)/shard_map/psum | solution.py:268
  589.8 2.5 copy-start.8
  662.4 2.7 copy-start.23
  662.4 3.6 copy-start.24
  662.4 4.3 copy-start.22
Sparse Core Ops, SparseCore 0:
  10.4 36.1 all-gather.5
  59.1 51.8 all-reduce.8
  113.0 34.6 all-gather.7
  149.6 35.2 all-gather.9
  191.6 51.8 all-reduce.10
  252.5 7.3 reduce-scatter.16
  262.2 9.1 reduce-scatter.18
  276.0 88.2 all-reduce.12
  368.0 26.6 reduce-scatter.22
  397.6 52.6 reduce-scatter.24
  453.5 52.6 reduce-scatter.26
  509.0 43.9 reduce-scatter.20
  556.3 23.6 reduce-scatter.28
  583.5 24.8 reduce-scatter.30
  611.6 24.7 reduce-scatter.32
  639.0 23.3 all-reduce.14
where the time goes:
time: 675 us; the launch traced here: 674 us
  waiting for transfers between devices  518 us (77%)
  blocking collectives  61.7 us (9%)
  matrix products  36.9 us (5%)
  local copies, waits for them, and re-layouts  25.3 us (4%)
  other arithmetic  16.3 us (2%)
  between operations  15.1 us (2%)
    psum x1, waiting for transfers between devices, per_device(): output = resid + lax.psum(mlp_terms, 'tp') + shifts_f[3]  73.8 us
    unnamed x19, waiting for transfers between devices  68.9 us
    reduce_scatter x1, waiting for transfers between devices, per_device(): lax.psum_scatter(grad_terms[3], 'dp', scatter_dimension=0, tiled=True)  55.9 us
    reduce_scatter x1, waiting for transfers between devices, per_device(): lax.psum_scatter(grad_terms[2], 'dp', scatter_dimension=0, tiled=True)  55.6 us
    psum x1, waiting for transfers between devices, per_device(): lax.psum(jnp.einsum('rf,df->rd', hidden_grad, w_fc, preferred_element_typ...  51.9 us
    reduce_scatter x1, waiting for transfers between devices, per_device(): lax.psum_scatter(grad_terms[0], 'dp', scatter_dimension=0, tiled=True)  46.8 us
    psum x1, waiting for transfers between devices, per_device(): resid = input_f32 + lax.psum(head_terms, 'tp') + shifts_f[2]  41.9 us
    all_gather x1, waiting for transfers between devices, per_device(): lax.all_gather(out_weight, 'dp', axis=0, tiled=True)  33.9 us
  transfers between devices with their start and end apart: 16, of which 14 were waited for; matrix products, arithmetic and copies ran while one was open for 6% of the time, Pallas kernels for 0%

commit v1 on v0

v1 whole, which is shorter than its diff:
```python
import functools

import jax
import jax.numpy as jnp
from jax import lax
from jax.experimental import pallas as pl
from jax.experimental.pallas import tpu as pltpu
from jax.sharding import PartitionSpec as P

EPSILON = 1e-05
MASKED_SCORE = -1e30
GELU_SCALE = 0.7978845608028654
F32, BF16 = jnp.float32, jnp.bfloat16
MESH = pl.DeviceIdType.MESH
TILE = 256


def normalize(values):
    centered = values - jnp.mean(values, axis=-1, keepdims=True)
    inverse = lax.rsqrt(jnp.mean(centered * centered, axis=-1, keepdims=True) + EPSILON)
    return centered * inverse, inverse


def norm_back(upstream, normed, inverse, gain_row):
    scaled = upstream * gain_row
    return inverse * (
        scaled
        - jnp.mean(scaled, axis=-1, keepdims=True)
        - normed * jnp.mean(scaled * normed, axis=-1, keepdims=True)
    )


def gelu_slope(pre_act):
    inner_arg = GELU_SCALE * (pre_act + 0.044715 * pre_act * pre_act * pre_act)
    tanh_val = jnp.tanh(inner_arg)
    activated = 0.5 * pre_act * (1.0 + tanh_val)
    slopes = 0.5 * (1.0 + tanh_val) + 0.5 * pre_act * (1.0 - tanh_val * tanh_val) * GELU_SCALE * (
        1.0 + 3.0 * 0.044715 * pre_act * pre_act
    )
    return (activated, slopes)


def dot_nn(a, b):
    return lax.dot_general(a, b, (((1,), (0,)), ((), ())), preferred_element_type=F32)


def dot_nt(a, b):
    return lax.dot_general(a, b, (((1,), (1,)), ((), ())), preferred_element_type=F32)


def dot_tn(a, b):
    return lax.dot_general(a, b, (((0,), (0,)), ((), ())), preferred_element_type=F32)


def loop(count, body):
    def step(j, carry):
        body(j)
        return carry

    lax.fori_loop(0, count, step, 0)


def tile_at(j, size=TILE):
    return pl.ds(pl.multiple_of(j * size, size), size)


def layer_kernel(
    nd, nt, head_dim,
    x_ref, gy_ref, small_ref, mask_ref, lq_ref, lp_ref, lf_ref, lo_ref,
    out_ref, ing_ref, gq_ref, gp_ref, gf_ref, go_ref, gs_ref,
    wq, wp, wf, wo, small_in, small_f, ln1_s, q_s, kv_s, prob_s, attn_s,
    part, rs_in, ag, resid_s, dact_s, act_s, dpre_s, dresid_s, dkv_own, dkv_out, dkv_in, st_s,
    loc_q, loc_p, loc_f, loc_o, par_q, par_p, par_f, par_o,
    sum_q, sum_p, sum_f, sum_o, rcv_q, rcv_p, rcv_f, rcv_o,
    tp_small, own_small, ctx_small, dp_small, send_sems, recv_sems,
):
    d, c, t = lax.axis_index("dp"), lax.axis_index("ctx"), lax.axis_index("tp")
    other = 1 - c
    rows, width = x_ref.shape
    local = q_s.shape[1]
    hidden = act_s.shape[1]
    heads = local // head_dim
    block = lq_ref.shape[0]
    half = block // 2
    own_rows = rows // nt
    scale = head_dim ** (-0.5)
    count = [0]
    pending = []

    def send(src, dst, **where):
        i = count[0]
        count[0] += 1
        copy = pltpu.make_async_remote_copy(
            src_ref=src, dst_ref=dst, send_sem=send_sems.at[i], recv_sem=recv_sems.at[i],
            device_id=where, device_id_type=MESH,
        )
        copy.start()
        pending.append(copy)
        return copy

    def dp_at(k):
        return lax.rem(d + k, nd)

    def tp_at(k):
        return lax.rem(t + k, nt)

    def mine(size=own_rows):
        return pl.ds(pl.multiple_of(t * size, size), size)

    barrier = pltpu.get_barrier_semaphore()
    for k in range(1, nd):
        pl.semaphore_signal(barrier, inc=1, device_id={"dp": dp_at(k)}, device_id_type=MESH)
    for k in range(1, nt):
        pl.semaphore_signal(barrier, inc=1, device_id={"tp": tp_at(k)}, device_id_type=MESH)
    pl.semaphore_signal(barrier, inc=1, device_id={"ctx": other}, device_id_type=MESH)
    pl.semaphore_wait(barrier, nd + nt - 1)

    small_copies = [send(small_ref, small_in.at[d], dp=dp_at(k)) for k in range(1, nd)]

    def half_at(owner, core):
        return pl.ds(pl.multiple_of(owner * block + core * half, half), half)

    def gather(shard, whole):
        return [
            send(shard.at[pl.ds(pl.multiple_of(c * half, half), half)], whole.at[half_at(d, c)],
                 dp=dp_at(k))
            for k in range(1, nd)
        ]

    def hand_on(whole, copies):
        handed = []
        for k in range(1, nd):
            copies[k - 1].wait_recv()
            place = whole.at[half_at(lax.rem(d - k + nd, nd), c)]
            handed.append(send(place, place, ctx=other))
        return handed

    def arrive(copies):
        for copy in copies:
            copy.wait_recv()

    got_q = gather(lq_ref, wq)
    got_p = gather(lp_ref, wp)
    got_f = gather(lf_ref, wf)
    got_o = gather(lo_ref, wo)
    own_block = pl.ds(pl.multiple_of(d * block, block), block)
    for shard, whole in ((lq_ref, wq), (lp_ref, wp), (lf_ref, wf), (lo_ref, wo)):
        whole[own_block, :] = shard[...]
    small_in[d] = small_ref[...]

    arrive(small_copies)
    total = small_in[0].astype(F32)
    for k in range(1, nd):
        total = total + small_in[k].astype(F32)
    small_f[...] = total

    def first_norm(j):
        at = tile_at(j, own_rows)
        normed, _ = normalize(x_ref[at, :].astype(F32))
        ln1_s[at, :] = (normed * small_f[0:1, :] + small_f[2:3, :]).astype(BF16)

    loop(nt, first_norm)
    handed = hand_on(wq, got_q)
    arrive(handed)
    kv_s[0:rows, 0:local] = dot_nn(ln1_s[...], wq[:, local : 2 * local]).astype(BF16)
    kv_s[0:rows, local : 2 * local] = (
        dot_nn(ln1_s[...], wq[:, 2 * local : 3 * local]) + small_f[7:8, local : 2 * local]
    ).astype(BF16)
    kv_copy = send(kv_s.at[pl.ds(0, rows)], kv_s.at[pl.ds(rows, rows)], ctx=other)
    q_s[...] = (dot_nn(ln1_s[...], wq[:, 0:local]) + small_f[7:8, 0:local]).astype(BF16)
    handed_p = hand_on(wp, got_p)
    kv_copy.wait_recv()

    mixed = []
    for h in range(heads):
        at = slice(h * head_dim, (h + 1) * head_dim)
        vat = slice(local + h * head_dim, local + (h + 1) * head_dim)
        scores = dot_nt(q_s[:, at], kv_s[:, at]) * scale + mask_ref[...].astype(F32)
        top = jnp.max(scores, axis=-1, keepdims=True)
        log_total = top + jnp.log(jnp.sum(jnp.exp(scores - top), axis=-1, keepdims=True))
        probs = jnp.exp(scores - log_total)
        prob_s[h] = probs
        mixed.append(dot_nn(probs.astype(BF16), kv_s[:, vat]))
    attn_s[...] = jnp.concatenate(mixed, axis=1).astype(BF16)

    def reduce_start(i):
        return [
            send(part.at[i, pl.ds(pl.multiple_of(tp_at(k) * own_rows, own_rows), own_rows)],
                 rs_in.at[i, k - 1], tp=tp_at(k))
            for k in range(1, nt)
        ]

    def reduce_end(i, copies):
        total = part[i, mine(), :].astype(F32)
        for k in range(1, nt):
            copies[k - 1].wait_recv()
            total = total + rs_in[i, k - 1].astype(F32)
        return total

    def share(i, value):
        ag[i, mine(), :] = value.astype(BF16)
        place = ag.at[i, mine()]
        return [send(place, place, tp=tp_at(k)) for k in range(1, nt)]

    arrive(handed_p)

    def proj_tile(j):
        part[0, :, tile_at(j)] = dot_nt(attn_s[...], wp[tile_at(j), :]).astype(BF16)

    loop(width // TILE, proj_tile)
    reduced = reduce_start(0)
    handed_f = hand_on(wf, got_f)
    own_x = x_ref[mine(), :].astype(F32)
    resid = own_x + reduce_end(0, reduced) + small_f[4:5, :]
    resid_s[...] = resid
    normed2, _ = normalize(resid)
    shared = share(0, normed2 * small_f[1:2, :] + small_f[3:4, :])
    handed_o = hand_on(wo, got_o)
    arrive(handed_f)
    arrive(handed_o)

    def dact_tile(j):
        dact_s[:, tile_at(j)] = dot_nn(gy_ref[...], wo[:, tile_at(j)])

    loop(hidden // TILE, dact_tile)
    arrive(shared)

    def hidden_tile(j):
        at = tile_at(j)
        pre = dot_nn(ag[0], wf[:, at]) + small_f[6:7, at]
        activated, slopes = gelu_slope(pre)
        act_s[:, at] = activated.astype(BF16)
        dpre = (dact_s[:, at] * slopes).astype(BF16)
        dpre_s[:, at] = dpre
        own_small[6:7, at] = jnp.sum(dpre.astype(F32), axis=0, keepdims=True)

    loop(hidden // TILE, hidden_tile)

    def dln2_tile(j):
        part[1, :, tile_at(j)] = dot_nt(dpre_s[...], wf[tile_at(j), :]).astype(BF16)

    loop(width // TILE, dln2_tile)
    reduced1 = reduce_start(1)

    def down_tile(j):
        part[2, :, tile_at(j)] = dot_nt(act_s[...], wo[tile_at(j), :]).astype(BF16)

    loop(width // TILE, down_tile)
    reduced2 = reduce_start(2)

    tile_rows = max(TILE, block)
    blocks_in = tile_rows // block

    def grad_start(left, right, grads, partner):
        def tile(j):
            value = dot_tn(left[:, tile_at(j, tile_rows)], right[...]).astype(BF16)
            grads[pl.ds(j * blocks_in, blocks_in)] = value.reshape(
                (blocks_in, 2, half, value.shape[1])
            )

        loop(width // tile_rows, tile)
        return send(grads.at[:, other], partner, ctx=other)

    def grad_spread(copy, grads, partner, sums, received):
        copy.wait_recv()

        def add(j):
            sums[j] = (grads[j, c].astype(F32) + partner[j].astype(F32)).astype(BF16)

        loop(nd, add)
        return [send(sums.at[dp_at(k)], received.at[k - 1], dp=dp_at(k)) for k in range(1, nd)]

    def grad_end(copies, sums, received, result):
        total = sums[d].astype(F32)
        for k in range(1, nd):
            copies[k - 1].wait_recv()
            total = total + received[k - 1].astype(F32)
        place = pl.ds(pl.multiple_of(c * half, half), half)
        result[place, :] = total
        return send(result.at[place], result.at[place], ctx=other)

    pair_o = grad_start(gy_ref, act_s, loc_o, par_o)

    dln2 = reduce_end(1, reduced1)
    normed2, inverse2 = normalize(resid_s[...])
    own_gy = gy_ref[mine(), :].astype(F32)
    dresid = own_gy + norm_back(dln2, normed2, inverse2, small_f[1:2, :])
    shared1 = share(1, dresid)
    dresid_s[...] = dresid
    tp_small[t, 1:2, :] = jnp.sum(dln2 * normed2, axis=0, keepdims=True)
    tp_small[t, 3:4, :] = jnp.sum(dln2, axis=0, keepdims=True)
    tp_small[t, 4:5, :] = jnp.sum(dresid, axis=0, keepdims=True)
    tp_small[t, 5:6, :] = jnp.sum(own_gy, axis=0, keepdims=True)
    spread_o = grad_spread(pair_o, loc_o, par_o, sum_o, rcv_o)
    pair_f = grad_start(ag.at[0], dpre_s, loc_f, par_f)
    arrive(shared1)
    shared2 = share(2, resid_s[...] + reduce_end(2, reduced2) + small_f[5:6, :])

    dattn = dot_nn(ag[1], wp[...]).astype(BF16)
    dq_parts, dk_parts, dv_parts = [], [], []
    for h in range(heads):
        at = slice(h * head_dim, (h + 1) * head_dim)
        vat = slice(local + h * head_dim, local + (h + 1) * head_dim)
        dattn_h = dattn[:, at]
        probs = prob_s[h]
        delta = jnp.sum(
            dattn_h.astype(F32) * attn_s[:, at].astype(F32), axis=-1, keepdims=True
        )
        dprob = dot_nt(dattn_h, kv_s[:, vat])
        dscore = (probs * (dprob - delta) * scale).astype(BF16)
        dq_parts.append(dot_nn(dscore, kv_s[:, at]))
        dk_parts.append(dot_tn(dscore, q_s[:, at]))
        dv_parts.append(dot_tn(probs.astype(BF16), dattn_h))
    dkv = jnp.concatenate(dk_parts + dv_parts, axis=1)
    dkv_out[...] = dkv[rows:, :]
    dkv_copy = send(dkv_out, dkv_in, ctx=other)
    dkv_own[...] = dkv[:rows, :]
    dq = jnp.concatenate(dq_parts, axis=1).astype(BF16)
    st_s[:, 0:local] = dq
    spread_f = grad_spread(pair_f, loc_f, par_f, sum_f, rcv_f)
    dkv_copy.wait_recv()
    st_s[:, local : 3 * local] = (dkv_own[...] + dkv_in[...]).astype(BF16)

    def dln1_tile(j):
        part[3, :, tile_at(j)] = dot_nt(st_s[...], wq[tile_at(j), :]).astype(BF16)

    loop(width // TILE, dln1_tile)
    reduced3 = reduce_start(3)
    pair_q = grad_start(ln1_s, st_s, loc_q, par_q)
    pair_p = grad_start(ag.at[1], attn_s, loc_p, par_p)
    own_small[7:8, :] = jnp.zeros((1, width), F32)
    own_small[7:8, 0:local] = jnp.sum(st_s[:, 0:local].astype(F32), axis=0, keepdims=True)
    own_small[7:8, local : 2 * local] = jnp.sum(
        st_s[:, 2 * local : 3 * local].astype(F32), axis=0, keepdims=True
    )
    spread_q = grad_spread(pair_q, loc_q, par_q, sum_q, rcv_q)
    spread_p = grad_spread(pair_p, loc_p, par_p, sum_p, rcv_p)

    dln1 = reduce_end(3, reduced3)
    normed1, inverse1 = normalize(x_ref[mine(), :].astype(F32))
    shared3 = share(3, dresid_s[...] + norm_back(dln1, normed1, inverse1, small_f[0:1, :]))
    tp_small[t, 0:1, :] = jnp.sum(dln1 * normed1, axis=0, keepdims=True)
    tp_small[t, 2:3, :] = jnp.sum(dln1, axis=0, keepdims=True)
    tp_small[t, 6:8, :] = jnp.zeros((2, width), F32)
    small_tp = [send(tp_small.at[t], tp_small.at[t], tp=tp_at(k)) for k in range(1, nt)]
    end_o = grad_end(spread_o, sum_o, rcv_o, go_ref)
    end_f = grad_end(spread_f, sum_f, rcv_f, gf_ref)
    arrive(small_tp)
    total = tp_small[0]
    for k in range(1, nt):
        total = total + tp_small[k]
    ctx_small[c, 0:6, :] = total[0:6]
    ctx_small[c, 6:8, :] = own_small[6:8, :]
    small_ctx = send(ctx_small.at[c], ctx_small.at[c], ctx=other)
    arrive(shared2)
    out_ref[...] = ag[2].astype(F32)
    small_ctx.wait_recv()
    dp_small[d] = ctx_small[0] + ctx_small[1]
    small_dp = [send(dp_small.at[d], dp_small.at[d], dp=dp_at(k)) for k in range(1, nd)]
    end_q = grad_end(spread_q, sum_q, rcv_q, gq_ref)
    end_p = grad_end(spread_p, sum_p, rcv_p, gp_ref)
    arrive(small_dp)
    total = dp_small[0]
    for k in range(1, nd):
        total = total + dp_small[k]
    gs_ref[...] = total
    arrive(shared3)
    ing_ref[...] = ag[3].astype(F32)
    arrive([end_o, end_f, end_q, end_p])
    for copy in pending:
        copy.wait_send()


def per_device(
    nd, nt,
    block_input, qkv_weight, qv_bias, proj_weight, fc_weight, fc_bias, out_weight,
    norm_gains, shifts, segment_ids, out_grad,
):
    d, c = lax.axis_index("dp"), lax.axis_index("ctx")
    rows, width = block_input.shape
    block, _, local = qkv_weight.shape
    hidden = fc_weight.shape[1]
    heads_here, head_part = qv_bias.shape[1:]
    head_dim = head_part * nd
    table_rows, table_part = fc_bias.shape
    seq_len = segment_ids.shape[1]
    half = block // 2
    own_rows = rows // nt

    def widen(shard, axis):
        shape = list(shard.shape)
        size = shape[axis]
        shape[axis] = size * nd
        start = [0] * len(shape)
        start[axis] = d * size
        return lax.dynamic_update_slice(jnp.zeros(shape, shard.dtype), shard, start)

    rows_of = [
        widen(norm_gains, 1),
        widen(shifts, 1),
        widen(fc_bias, 1).reshape(1, hidden),
        jnp.pad(widen(qv_bias, 2).reshape(1, 2 * local), ((0, 0), (0, width - 2 * local))),
        jnp.zeros((8, width), BF16),
    ]
    small = jnp.concatenate(rows_of, axis=0)

    seg = segment_ids[0]
    pos = jnp.arange(rows, dtype=jnp.int32)
    q_pos = c * rows + pos
    k_pos = jnp.concatenate([q_pos, (1 - c) * rows + pos])
    seg_q = lax.dynamic_slice_in_dim(seg, c * rows, rows)
    seg_k = jnp.concatenate([seg_q, lax.dynamic_slice_in_dim(seg, (1 - c) * rows, rows)])
    live = (seg_q[:, None] == seg_k[None, :]) & (k_pos[None, :] <= q_pos[:, None])
    mask = jnp.where(live, 0.0, MASKED_SCORE).astype(BF16)

    widths = (3 * local, local, hidden, hidden)
    vmem = pltpu.VMEM
    scratch = (
        [vmem((width, w), BF16) for w in widths]
        + [
            vmem((nd, 16, width), BF16),
            vmem((16, width), F32),
            vmem((rows, width), BF16),
            vmem((rows, local), BF16),
            vmem((2 * rows, 2 * local), BF16),
            vmem((heads_here, rows, 2 * rows), F32),
            vmem((rows, local), BF16),
            vmem((4, rows, width), BF16),
            vmem((4, nt - 1, own_rows, width), BF16),
            vmem((4, rows, width), BF16),
            vmem((own_rows, width), F32),
            vmem((rows, hidden), F32),
            vmem((rows, hidden), BF16),
            vmem((rows, hidden), BF16),
            vmem((own_rows, width), F32),
            vmem((rows, 2 * local), F32),
            vmem((rows, 2 * local), F32),
            vmem((rows, 2 * local), F32),
            vmem((rows, 3 * local), BF16),
        ]
        + [vmem((nd, 2, half, w), BF16) for w in widths]
        + [vmem((nd, half, w), BF16) for w in widths]
        + [vmem((nd, half, w), BF16) for w in widths]
        + [vmem((nd - 1, half, w), BF16) for w in widths]
        + [
            vmem((nt, 8, width), F32),
            vmem((8, width), F32),
            vmem((2, 8, width), F32),
            vmem((nd, 8, width), F32),
            pltpu.SemaphoreType.DMA((14 * (nd - 1) + 10 * (nt - 1) + 16,)),
            pltpu.SemaphoreType.DMA((14 * (nd - 1) + 10 * (nt - 1) + 16,)),
        ]
    )
    whole = pl.BlockSpec(memory_space=pltpu.VMEM)
    out_shapes = [
        (rows, width), (rows, width), (block, 3 * local), (block, local),
        (block, hidden), (block, hidden), (8, width),
    ]
    output, input_grad, g_qkv, g_proj, g_fc, g_out, g_small = pl.pallas_call(
        functools.partial(layer_kernel, nd, nt, head_dim),
        out_shape=[jax.ShapeDtypeStruct(shape, F32) for shape in out_shapes],
        in_specs=[whole] * 8,
        out_specs=[whole] * 7,
        scratch_shapes=scratch,
        compiler_params=pltpu.CompilerParams(
            collective_id=0, has_side_effects=True, vmem_limit_bytes=60 * 1024 * 1024
        ),
    )(
        block_input, out_grad, small, mask, qkv_weight.reshape(block, 3 * local),
        proj_weight, fc_weight, out_weight,
    )

    part_of = functools.partial(lax.dynamic_slice_in_dim, g_small, d * block, block, 1)()
    g_gains, g_shifts = part_of[0:2], part_of[2:6]
    g_fc_bias = lax.dynamic_slice_in_dim(
        g_small[6].reshape(table_rows, table_part * nd), d * table_part, table_part, 1
    )
    g_qv = lax.dynamic_slice_in_dim(
        g_small[7, : 2 * local].reshape(2, heads_here, head_dim), d * head_part, head_part, 2
    )
    return (
        output, input_grad, g_qkv.reshape(block, 3, local), g_qv, g_proj, g_fc, g_fc_bias,
        g_out, g_gains, g_shifts,
    )


def solution(mesh):
    in_specs = (
        P(("dp", "ctx"), None),
        P("dp", None, "tp"),
        P(None, "tp", "dp"),
        P("dp", "tp"),
        P("dp", "tp"),
        P("tp", "dp"),
        P("dp", "tp"),
        P(None, "dp"),
        P(None, "dp"),
        P("dp", None),
        P(("dp", "ctx"), None),
    )
    out_specs = (
        P(("dp", "ctx"), None),
        P(("dp", "ctx"), None),
        P("dp", None, "tp"),
        P(None, "tp", "dp"),
        P("dp", "tp"),
        P("dp", "tp"),
        P("tp", "dp"),
        P("dp", "tp"),
        P(None, "dp"),
        P(None, "dp"),
    )
    return jax.shard_map(
        functools.partial(per_device, mesh.shape["dp"], mesh.shape["tp"]),
        mesh=mesh, in_specs=in_specs, out_specs=out_specs, check_vma=False,
    )
```

time: 675 us -> 158 us (0.23)
  waiting for transfers between devices: 518 us -> 0 us
  Pallas kernels: 0 us -> 136 us
  blocking collectives: 61.7 us -> 0 us
  matrix products: 36.9 us -> 0 us
  other arithmetic: 16.3 us -> 0.87 us
  between operations: 15.1 us -> 0.73 us
    reduce_scatter x6 -> x0, waiting for transfers between devices: 193 us -> none  [the longest x1 55.9 us: per_device(): lax.psum_scatter(grad_terms[3], 'dp', scatter_dimension=0, tiled=True)]
    psum x4 -> x0, waiting for transfers between devices: 189 us -> none  [the longest x1 73.8 us: per_device(): output = resid + lax.psum(mlp_terms, 'tp') + shifts_f[3]]
    pallas_call x0 -> x1, Pallas kernels: none -> 136 us  [per_device(): pl.pallas_call(functools.partial(layer_kernel, nd, nt, head_dim), out_sha...]
    unnamed x19 -> x0, waiting for transfers between devices: 68.9 us -> none
    all_gather x3 -> x0, waiting for transfers between devices: 67.6 us -> none  [the longest x1 33.9 us: per_device(): lax.all_gather(out_weight, 'dp', axis=0, tiled=True)]
    all_gather x7 -> x0, blocking collectives: 48.9 us -> none  [the longest x1 12 us: per_device(): lax.all_gather(proj_weight, 'dp', axis=0, tiled=True)]
    dot_general x18 -> x0, matrix products: 36.9 us -> none  [the longest x1 4.02 us: per_device(): jnp.einsum('rf,df->rd', act_b, w_out, preferred_element_type=jnp.float32)]
    unnamed x106 -> x20, local copies, waits for them, and re-layouts: 19.4 us -> 7.3 us
  transfers between devices with their start and end apart: 16 -> 0, of which waited for: 14 -> 0; matrix products, arithmetic and copies ran while one was open for 6% -> 0% of each run, Pallas kernels for 0% -> 0%
where the time goes in v1:
time: 158 us
  Pallas kernels  136 us (86%)
  local copies, waits for them, and re-layouts  20.2 us (13%)
    pallas_call x1, Pallas kernels, per_device(): pl.pallas_call(functools.partial(layer_kernel, nd, nt, head_dim), out_sha...  136 us
    unnamed x20, local copies, waits for them, and re-layouts  7.3 us

profile of v1, /device:TPU:0, one launch (start us, length us, event | category | flops | bytes accessed | tf_op | source)
XLA Modules:
  0.0 157.6 jit_solution(6244587621055286818)
XLA Ops:
  0.6 0.0 copy-start.4
  0.7 0.7 constant_dynamic-slice_fusion.4
  1.4 0.9 select_convert_fusion.mask_ref
  2.3 0.7 constant_dynamic-update-slice_fusion
  3.0 0.7 constant_dynamic-update-slice_fusion.1
  3.7 0.8 dynamic_update_slice.15
  4.5 0.1 reshape.43
  4.6 0.8 dynamic_update_slice.14
  5.4 1.2 concatenate.9.small_ref
  6.6 0.0 copy-done.4
  6.6 0.2 copy.23
  6.8 0.9 copy.24.lq_ref
  7.7 135.8 %shard_map.186 = (f32[256,1024]{1,0:T(8,128)}, f32[256,1024]{1,0:T(8,128)}, f32[256,768]{1,0:T(8,128)}, f32[256,256]{1,0:T(8,128)}, f32[256,1024]{1,0:T(8,128)}, /*index=5*/f32[256,1024]{1,0:T(8,128)}, f32[8,1024]{1,0:T(8,128)}) custom-call(bf16[256,1024]{1,0:T(8,128)(2,1)} %x_ref.1, bf16[256,1024]{1,0:T(8,128)(2,1)} %gy_ref.1, ...), custom_call_target="tpu_custom_call" | custom-call | tf_op jit(solution)/shard_map/pallas_call | solution.py:459
  143.5 1.4 copy.25
  144.9 0.0 copy-start.3
  144.9 1.1 copy.26
  146.1 0.7 slice_reduce_fusion
  146.8 0.1 reshape_squeeze.6
  146.9 0.7 constant_dynamic-slice_fusion.2
  147.5 0.8 slice.13
  148.3 0.7 constant_dynamic-slice_fusion.1
  149.0 1.4 dynamic-slice.3
  150.3 1.3 constant_dynamic-slice_fusion
  151.6 0.0 copy-done.3
  151.6 0.0 copy-start.2
  151.6 1.0 copy.39
  152.6 0.6 copy-done.2
  153.2 0.0 copy-start.5
  153.2 0.0 copy-start.1
  153.2 1.0 copy.40
  154.2 0.1 copy-done.5
  154.3 0.7 copy.41
  155.0 0.0 copy-done.1
  155.0 0.0 copy-start
  155.0 1.0 copy.42
  156.0 0.6 copy-done
  156.6 1.0 copy.43
  (10 shorter events, 0.1 us)
Async XLA Ops:
  0.6 6.0 %copy-start.4 = (bf16[256,3,256]{2,0,1:T(8,128)(2,1)S(1)}, bf16[256,3,256]{2,0,1:T(8,128)(2,1)}, u32[]{:S(2)}) copy-start(bf16[256,3,256]{2,0,1:T(8,128)(2,1)} %param.12) | copy-start | bytes 1179652
  144.9 6.7 %copy-start.3 = (f32[256,1024]{1,0:T(8,128)S(1)}, f32[256,1024]{1,0:T(8,128)}, u32[]{:S(2)}) copy-start(f32[256,1024]{1,0:T(8,128)} %get-tuple-element.58) | copy-start | bytes 3145732
  151.6 1.6 %copy-start.2 = (f32[256,1024]{1,0:T(8,128)S(1)}, f32[256,1024]{1,0:T(8,128)}, u32[]{:S(2)}) copy-start(f32[256,1024]{1,0:T(8,128)} %get-tuple-element.59) | copy-start | bytes 3145732
  153.2 1.1 copy-start.5
  153.2 1.8 %copy-start.1 = (f32[256,1024]{1,0:T(8,128)S(1)}, f32[256,1024]{1,0:T(8,128)}, u32[]{:S(2)}) copy-start(f32[256,1024]{1,0:T(8,128)} %get-tuple-element.63) | copy-start | bytes 3145732
  155.0 1.6 %copy-start = (f32[256,1024]{1,0:T(8,128)S(1)}, f32[256,1024]{1,0:T(8,128)}, u32[]{:S(2)}) copy-start(f32[256,1024]{1,0:T(8,128)} %get-tuple-element.65) | copy-start | bytes 3145732

commit v2 on v1

--- a/solution.py
+++ b/solution.py
@@ -66,9 +66,9 @@
 
 def layer_kernel(
     nd, nt, head_dim,
-    x_ref, gy_ref, small_ref, mask_ref, lq_ref, lp_ref, lf_ref, lo_ref,
-    out_ref, ing_ref, gq_ref, gp_ref, gf_ref, go_ref, gs_ref,
-    wq, wp, wf, wo, small_in, small_f, ln1_s, q_s, kv_s, prob_s, attn_s,
+    x_ref, gy_ref, gains_ref, shifts_ref, fcb_ref, qvb_ref, seg_ref, lq_ref, lp_ref, lf_ref, lo_ref,
+    out_ref, ing_ref, gq_ref, gp_ref, gf_ref, go_ref, ggains_ref, gshifts_ref, gfcb_ref, gqvb_ref,
+    wq, wp, wf, wo, small_in, small_f, mask_ref, ln1_s, q_s, kv_s, prob_s, attn_s,
     part, rs_in, ag, resid_s, dact_s, act_s, dpre_s, dresid_s, dkv_own, dkv_out, dkv_in, st_s,
     loc_q, loc_p, loc_f, loc_o, par_q, par_p, par_f, par_o,
     sum_q, sum_p, sum_f, sum_o, rcv_q, rcv_p, rcv_f, rcv_o,
@@ -115,7 +115,15 @@
     pl.semaphore_signal(barrier, inc=1, device_id={"ctx": other}, device_id_type=MESH)
     pl.semaphore_wait(barrier, nd + nt - 1)
 
-    small_copies = [send(small_ref, small_in.at[d], dp=dp_at(k)) for k in range(1, nd)]
+    def place(shard):
+        size = shard.shape[1]
+        lanes = lax.broadcasted_iota(jnp.int32, (shard.shape[0], size * nd), 1)
+        spread = jnp.concatenate([shard.astype(F32)] * nd, axis=1)
+        return jnp.where((lanes >= d * size) & (lanes < (d + 1) * size), spread, 0.0)
+
+    def in_a_row(tables):
+        return jnp.concatenate([tab[r : r + 1] for tab in tables for r in range(tab.shape[0])], axis=1)
+
 
     def half_at(owner, core):
         return pl.ds(pl.multiple_of(owner * block + core * half, half), half)
@@ -143,15 +151,27 @@
     got_p = gather(lp_ref, wp)
     got_f = gather(lf_ref, wf)
     got_o = gather(lo_ref, wo)
+    small_in[d, 0:2, :] = place(gains_ref[...])
+    small_in[d, 2:6, :] = place(shifts_ref[...])
+    small_in[d, 6:7, :] = in_a_row([place(fcb_ref[...])])
+    small_in[d, 7:8, :] = jnp.zeros((1, width), F32)
+    small_in[d, 7:8, 0 : 2 * local] = in_a_row([place(qvb_ref[m]) for m in range(2)])
+    small_copies = [send(small_in.at[d], small_in.at[d], dp=dp_at(k)) for k in range(1, nd)]
+    seg_own = seg_ref[:, pl.ds(pl.multiple_of(c * rows, rows), rows)].astype(F32)
+    seg_rest = seg_ref[:, pl.ds(pl.multiple_of(other * rows, rows), rows)].astype(F32)
+    seg_column = jnp.transpose(jnp.broadcast_to(seg_own, (128, rows)))[:, 0:1]
+    seg_keys = jnp.concatenate([seg_own, seg_rest], axis=1)
+    q_pos = c * rows + lax.broadcasted_iota(jnp.int32, (rows, 2 * rows), 0)
+    lane = lax.broadcasted_iota(jnp.int32, (rows, 2 * rows), 1)
+    k_pos = lane + jnp.where(lane < rows, c * rows, other * rows - rows)
+    mask_ref[...] = jnp.where((seg_column == seg_keys) & (k_pos <= q_pos), 0.0, MASKED_SCORE)
     own_block = pl.ds(pl.multiple_of(d * block, block), block)
     for shard, whole in ((lq_ref, wq), (lp_ref, wp), (lf_ref, wf), (lo_ref, wo)):
         whole[own_block, :] = shard[...]
-    small_in[d] = small_ref[...]
-
     arrive(small_copies)
-    total = small_in[0].astype(F32)
+    total = small_in[0]
     for k in range(1, nd):
-        total = total + small_in[k].astype(F32)
+        total = total + small_in[k]
     small_f[...] = total
 
     def first_norm(j):
@@ -175,7 +195,7 @@
     for h in range(heads):
         at = slice(h * head_dim, (h + 1) * head_dim)
         vat = slice(local + h * head_dim, local + (h + 1) * head_dim)
-        scores = dot_nt(q_s[:, at], kv_s[:, at]) * scale + mask_ref[...].astype(F32)
+        scores = dot_nt(q_s[:, at], kv_s[:, at]) * scale + mask_ref[...]
         top = jnp.max(scores, axis=-1, keepdims=True)
         log_total = top + jnp.log(jnp.sum(jnp.exp(scores - top), axis=-1, keepdims=True))
         probs = jnp.exp(scores - log_total)
@@ -246,7 +266,6 @@
         part[2, :, tile_at(j)] = dot_nt(act_s[...], wo[tile_at(j), :]).astype(BF16)
 
     loop(width // TILE, down_tile)
-    reduced2 = reduce_start(2)
 
     tile_rows = max(TILE, block)
     blocks_in = tile_rows // block
@@ -286,6 +305,7 @@
     own_gy = gy_ref[mine(), :].astype(F32)
     dresid = own_gy + norm_back(dln2, normed2, inverse2, small_f[1:2, :])
     shared1 = share(1, dresid)
+    reduced2 = reduce_start(2)
     dresid_s[...] = dresid
     tp_small[t, 1:2, :] = jnp.sum(dln2 * normed2, axis=0, keepdims=True)
     tp_small[t, 3:4, :] = jnp.sum(dln2, axis=0, keepdims=True)
@@ -294,7 +314,6 @@
     spread_o = grad_spread(pair_o, loc_o, par_o, sum_o, rcv_o)
     pair_f = grad_start(ag.at[0], dpre_s, loc_f, par_f)
     arrive(shared1)
-    shared2 = share(2, resid_s[...] + reduce_end(2, reduced2) + small_f[5:6, :])
 
     dattn = dot_nn(ag[1], wp[...]).astype(BF16)
     dq_parts, dk_parts, dv_parts = [], [], []
@@ -336,6 +355,7 @@
     spread_q = grad_spread(pair_q, loc_q, par_q, sum_q, rcv_q)
     spread_p = grad_spread(pair_p, loc_p, par_p, sum_p, rcv_p)
 
+    shared2 = share(2, resid_s[...] + reduce_end(2, reduced2) + small_f[5:6, :])
     dln1 = reduce_end(3, reduced3)
     normed1, inverse1 = normalize(x_ref[mine(), :].astype(F32))
     shared3 = share(3, dresid_s[...] + norm_back(dln1, normed1, inverse1, small_f[0:1, :]))
@@ -363,7 +383,25 @@
     total = dp_small[0]
     for k in range(1, nd):
         total = total + dp_small[k]
-    gs_ref[...] = total
+
+    def own_part(table):
+        size = table.shape[1] // nd
+        part_here = jnp.zeros((table.shape[0], size), F32)
+        for k in range(nd):
+            part_here = jnp.where(d == k, table[:, k * size : (k + 1) * size], part_here)
+        return part_here
+
+    def as_table(row, columns, count):
+        return jnp.concatenate(
+            [row[:, r * columns : (r + 1) * columns] for r in range(count)], axis=0
+        )
+
+    ggains_ref[...] = own_part(total[0:2])
+    gshifts_ref[...] = own_part(total[2:6])
+    table_rows = fcb_ref.shape[0]
+    gfcb_ref[...] = own_part(as_table(total[6:7], hidden // table_rows, table_rows))
+    for m in range(2):
+        gqvb_ref[m] = own_part(as_table(total[7:8, m * local : (m + 1) * local], head_dim, heads))
     arrive(shared3)
     ing_ref[...] = ag[3].astype(F32)
     arrive([end_o, end_f, end_q, end_p])
@@ -371,55 +409,35 @@
         copy.wait_send()
 
 
+def move_kernel(count, *refs):
+    sems = refs[2 * count]
+    copies = [pltpu.make_async_copy(refs[i], refs[count + i], sems.at[i]) for i in range(count)]
+    for copy in copies:
+        copy.start()
+    for copy in copies:
+        copy.wait()
+
+
 def per_device(
     nd, nt,
     block_input, qkv_weight, qv_bias, proj_weight, fc_weight, fc_bias, out_weight,
     norm_gains, shifts, segment_ids, out_grad,
 ):
-    d, c = lax.axis_index("dp"), lax.axis_index("ctx")
     rows, width = block_input.shape
     block, _, local = qkv_weight.shape
     hidden = fc_weight.shape[1]
     heads_here, head_part = qv_bias.shape[1:]
     head_dim = head_part * nd
-    table_rows, table_part = fc_bias.shape
-    seq_len = segment_ids.shape[1]
     half = block // 2
     own_rows = rows // nt
-
-    def widen(shard, axis):
-        shape = list(shard.shape)
-        size = shape[axis]
-        shape[axis] = size * nd
-        start = [0] * len(shape)
-        start[axis] = d * size
-        return lax.dynamic_update_slice(jnp.zeros(shape, shard.dtype), shard, start)
-
-    rows_of = [
-        widen(norm_gains, 1),
-        widen(shifts, 1),
-        widen(fc_bias, 1).reshape(1, hidden),
-        jnp.pad(widen(qv_bias, 2).reshape(1, 2 * local), ((0, 0), (0, width - 2 * local))),
-        jnp.zeros((8, width), BF16),
-    ]
-    small = jnp.concatenate(rows_of, axis=0)
-
-    seg = segment_ids[0]
-    pos = jnp.arange(rows, dtype=jnp.int32)
-    q_pos = c * rows + pos
-    k_pos = jnp.concatenate([q_pos, (1 - c) * rows + pos])
-    seg_q = lax.dynamic_slice_in_dim(seg, c * rows, rows)
-    seg_k = jnp.concatenate([seg_q, lax.dynamic_slice_in_dim(seg, (1 - c) * rows, rows)])
-    live = (seg_q[:, None] == seg_k[None, :]) & (k_pos[None, :] <= q_pos[:, None])
-    mask = jnp.where(live, 0.0, MASKED_SCORE).astype(BF16)
-
     widths = (3 * local, local, hidden, hidden)
     vmem = pltpu.VMEM
     scratch = (
         [vmem((width, w), BF16) for w in widths]
         + [
-            vmem((nd, 16, width), BF16),
-            vmem((16, width), F32),
+            vmem((nd, 8, width), F32),
+            vmem((8, width), F32),
+            vmem((rows, 2 * rows), F32),
             vmem((rows, width), BF16),
             vmem((rows, local), BF16),
             vmem((2 * rows, 2 * local), BF16),
@@ -453,35 +471,33 @@
     )
     whole = pl.BlockSpec(memory_space=pltpu.VMEM)
     out_shapes = [
-        (rows, width), (rows, width), (block, 3 * local), (block, local),
-        (block, hidden), (block, hidden), (8, width),
+        (rows, width), (rows, width), (block, 3 * local), (block, local), (block, hidden),
+        (block, hidden), norm_gains.shape, shifts.shape, fc_bias.shape, qv_bias.shape,
     ]
-    output, input_grad, g_qkv, g_proj, g_fc, g_out, g_small = pl.pallas_call(
+    results = pl.pallas_call(
         functools.partial(layer_kernel, nd, nt, head_dim),
         out_shape=[jax.ShapeDtypeStruct(shape, F32) for shape in out_shapes],
-        in_specs=[whole] * 8,
-        out_specs=[whole] * 7,
+        in_specs=[whole] * 11,
+        out_specs=[whole] * 10,
         scratch_shapes=scratch,
         compiler_params=pltpu.CompilerParams(
             collective_id=0, has_side_effects=True, vmem_limit_bytes=60 * 1024 * 1024
         ),
     )(
-        block_input, out_grad, small, mask, qkv_weight.reshape(block, 3 * local),
-        proj_weight, fc_weight, out_weight,
-    )
-
-    part_of = functools.partial(lax.dynamic_slice_in_dim, g_small, d * block, block, 1)()
-    g_gains, g_shifts = part_of[0:2], part_of[2:6]
-    g_fc_bias = lax.dynamic_slice_in_dim(
-        g_small[6].reshape(table_rows, table_part * nd), d * table_part, table_part, 1
-    )
-    g_qv = lax.dynamic_slice_in_dim(
-        g_small[7, : 2 * local].reshape(2, heads_here, head_dim), d * head_part, head_part, 2
-    )
-    return (
-        output, input_grad, g_qkv.reshape(block, 3, local), g_qv, g_proj, g_fc, g_fc_bias,
-        g_out, g_gains, g_shifts,
-    )
+        block_input, out_grad, norm_gains, shifts, fc_bias, qv_bias, segment_ids,
+        qkv_weight.reshape(block, 3 * local), proj_weight, fc_weight, out_weight,
+    )
+    g_qkv = results[2].reshape(block, 3, local)
+    plain = results[:2] + results[3:]
+    anywhere = pl.BlockSpec(memory_space=pl.ANY)
+    output, input_grad, g_proj, g_fc, g_out, g_gains, g_shifts, g_fc_bias, g_qv = pl.pallas_call(
+        functools.partial(move_kernel, len(plain)),
+        out_shape=[jax.ShapeDtypeStruct(array.shape, F32) for array in plain],
+        in_specs=[anywhere] * len(plain),
+        out_specs=[anywhere] * len(plain),
+        scratch_shapes=[pltpu.SemaphoreType.DMA((len(plain),))],
+    )(*plain)
+    return (output, input_grad, g_qkv, g_qv, g_proj, g_fc, g_fc_bias, g_out, g_gains, g_shifts)
 
 
 def solution(mesh):

time: 158 us -> 299 us (1.89)
  Pallas kernels: 136 us -> 294 us
  local copies, waits for them, and re-layouts: 20.2 us -> 3.5 us
    pallas_call x0 -> x1, Pallas kernels: none -> 137 us  [per_device(): pl.pallas_call(functools.partial(move_kernel, len(plain)), out_shape=[jax...]
    pallas_call x1, Pallas kernels: 136 us -> 158 us  [per_device(): pl.pallas_call(functools.partial(layer_kernel, nd, nt, head_dim), out_sha...]
    unnamed x20 -> x4, local copies, waits for them, and re-layouts: 7.3 us -> 2.32 us
    slice x4 -> x0, local copies, waits for them, and re-layouts: 4.13 us -> none  [the longest x2 2.64 us: per_device(): g_gains, g_shifts = (part_of[0:2], part_of[2:6])]
where the time goes in v2:
time: 299 us; the launch traced here: 298 us
  Pallas kernels  294 us (98%)
  local copies, waits for them, and re-layouts  3.5 us (1%)
    pallas_call x1, Pallas kernels, per_device(): pl.pallas_call(functools.partial(layer_kernel, nd, nt, head_dim), out_sha...  158 us
    pallas_call x1, Pallas kernels, per_device(): pl.pallas_call(functools.partial(move_kernel, len(plain)), out_shape=[jax...  137 us

profile of v2, /device:TPU:0, one launch (start us, length us, event | category | flops | bytes accessed | tf_op | source)
XLA Modules:
  0.0 298.4 jit_solution(14042607194092994074)
XLA Ops:
  0.6 1.2 copy.23
  1.8 0.9 copy.24.lq_ref
  2.7 157.6 %shard_map.186 = (f32[256,1024]{1,0:T(8,128)}, f32[256,1024]{1,0:T(8,128)}, f32[256,768]{1,0:T(8,128)}, f32[256,256]{1,0:T(8,128)}, f32[256,1024]{1,0:T(8,128)},...) custom-call(bf16[256,1024]{1,0:T(8,128)(2,1)} %x_ref.1, ...), custom_call_target="tpu_custom_call" | custom-call | tf_op jit(solution)/shard_map/pallas_call | solution.py:477
  160.3 0.0 copy-start
  160.3 136.6 %shard_map.187 = (f32[256,1024]{1,0:T(8,128)}, f32[256,1024]{1,0:T(8,128)}, f32[256,256]{1,0:T(8,128)}, f32[256,1024]{1,0:T(8,128)}, f32[256,1024]{1,0:T(8,128)}...) custom-call(f32[256,1024]{1,0:T(8,128)} %get-tuple-element.29.refs_0_, ...), custom_call_target="tpu_custom_call" | custom-call | tf_op jit(solution)/shard_map/pallas_call | solution.py:493
  296.9 0.0 copy-done
  297.0 0.3 copy.25
  297.2 1.1 copy.26
Async XLA Ops:
  160.3 136.6 %copy-start = (f32[256,768]{1,0:T(8,128)S(1)}, f32[256,768]{1,0:T(8,128)}, u32[]{:S(2)}) copy-start(f32[256,768]{1,0:T(8,128)} %get-tuple-element.40) | copy-start | bytes 2359300

commit v3 on v2

--- a/solution.py
+++ b/solution.py
@@ -147,16 +147,16 @@
         for copy in copies:
             copy.wait_recv()
 
-    got_q = gather(lq_ref, wq)
-    got_p = gather(lp_ref, wp)
-    got_f = gather(lf_ref, wf)
-    got_o = gather(lo_ref, wo)
     small_in[d, 0:2, :] = place(gains_ref[...])
     small_in[d, 2:6, :] = place(shifts_ref[...])
     small_in[d, 6:7, :] = in_a_row([place(fcb_ref[...])])
     small_in[d, 7:8, :] = jnp.zeros((1, width), F32)
     small_in[d, 7:8, 0 : 2 * local] = in_a_row([place(qvb_ref[m]) for m in range(2)])
     small_copies = [send(small_in.at[d], small_in.at[d], dp=dp_at(k)) for k in range(1, nd)]
+    got_q = gather(lq_ref, wq)
+    got_p = gather(lp_ref, wp)
+    got_f = gather(lf_ref, wf)
+    got_o = gather(lo_ref, wo)
     seg_own = seg_ref[:, pl.ds(pl.multiple_of(c * rows, rows), rows)].astype(F32)
     seg_rest = seg_ref[:, pl.ds(pl.multiple_of(other * rows, rows), rows)].astype(F32)
     seg_column = jnp.transpose(jnp.broadcast_to(seg_own, (128, rows)))[:, 0:1]
@@ -407,15 +407,6 @@
     arrive([end_o, end_f, end_q, end_p])
     for copy in pending:
         copy.wait_send()
-
-
-def move_kernel(count, *refs):
-    sems = refs[2 * count]
-    copies = [pltpu.make_async_copy(refs[i], refs[count + i], sems.at[i]) for i in range(count)]
-    for copy in copies:
-        copy.start()
-    for copy in copies:
-        copy.wait()
 
 
 def per_device(
@@ -488,15 +479,7 @@
         qkv_weight.reshape(block, 3 * local), proj_weight, fc_weight, out_weight,
     )
     g_qkv = results[2].reshape(block, 3, local)
-    plain = results[:2] + results[3:]
-    anywhere = pl.BlockSpec(memory_space=pl.ANY)
-    output, input_grad, g_proj, g_fc, g_out, g_gains, g_shifts, g_fc_bias, g_qv = pl.pallas_call(
-        functools.partial(move_kernel, len(plain)),
-        out_shape=[jax.ShapeDtypeStruct(array.shape, F32) for array in plain],
-        in_specs=[anywhere] * len(plain),
-        out_specs=[anywhere] * len(plain),
-        scratch_shapes=[pltpu.SemaphoreType.DMA((len(plain),))],
-    )(*plain)
+    output, input_grad, _, g_proj, g_fc, g_out, g_gains, g_shifts, g_fc_bias, g_qv = results
     return (output, input_grad, g_qkv, g_qv, g_proj, g_fc, g_fc_bias, g_out, g_gains, g_shifts)
 
 

time: 299 us -> 148 us (0.49)
  Pallas kernels: 294 us -> 134 us
  local copies, waits for them, and re-layouts: 3.5 us -> 12.5 us
    pallas_call x1 -> x0, Pallas kernels: 137 us -> none  [per_device(): pl.pallas_call(functools.partial(move_kernel, len(plain)), out_shape=[jax...]
    pallas_call x1, Pallas kernels: 158 us -> 134 us  [per_device(): pl.pallas_call(functools.partial(layer_kernel, nd, nt, head_dim), out_sha...]
    unnamed x4 -> x29, local copies, waits for them, and re-layouts: 2.32 us -> 10.2 us
where the time goes in v3:
time: 148 us; the launch traced here: 147 us
  Pallas kernels  134 us (91%)
  local copies, waits for them, and re-layouts  12.5 us (8%)
    pallas_call x1, Pallas kernels, per_device(): pl.pallas_call(functools.partial(layer_kernel, nd, nt, head_dim), out_sha...  134 us
    unnamed x29, local copies, waits for them, and re-layouts  10.2 us

profile of v3, /device:TPU:0, one launch (start us, length us, event | category | flops | bytes accessed | tf_op | source)
XLA Modules:
  0.0 147.3 jit_solution(16893587640183650691)
XLA Ops:
  0.6 1.2 copy.23
  1.8 0.9 copy.24.lq_ref
  2.7 134.1 %shard_map.186 = (f32[256,1024]{1,0:T(8,128)}, f32[256,1024]{1,0:T(8,128)}, f32[256,768]{1,0:T(8,128)}, f32[256,256]{1,0:T(8,128)}, f32[256,1024]{1,0:T(8,128)},...) custom-call(bf16[256,1024]{1,0:T(8,128)(2,1)} %x_ref.1, ...), custom_call_target="tpu_custom_call" | custom-call | tf_op jit(solution)/shard_map/pallas_call | solution.py:468
  136.9 1.4 copy.25
  138.3 0.0 copy-start.3
  138.3 1.1 copy.26
  139.4 0.1 copy-done.3
  139.6 0.0 copy-start.2
  139.6 1.0 copy.36
  140.5 0.6 copy-done.2
  141.2 0.0 copy-start.7
  141.2 0.0 copy-start.4
  141.2 0.0 copy-start.1
  141.2 1.0 copy.37
  142.1 0.0 copy-done.7
  142.1 0.6 copy.38
  142.7 0.0 copy-done.4
  142.7 0.7 copy.39
  143.4 0.0 copy-done.1
  143.4 0.0 copy-start.6
  143.4 0.0 copy-start
  143.4 1.0 copy.40
  144.4 0.0 copy-done.6
  144.4 0.6 copy.41
  145.0 0.0 copy-done
  145.0 0.0 copy-start.8
  145.1 1.0 copy.42
  146.0 0.0 copy-done.8
  146.0 0.0 copy-start.5
  146.0 0.6 copy.43
  146.6 0.1 copy-done.5
  146.7 0.6 copy.44
Async XLA Ops:
  138.3 1.3 copy-start.3
  139.6 1.6 %copy-start.2 = (f32[256,1024]{1,0:T(8,128)S(1)}, f32[256,1024]{1,0:T(8,128)}, u32[]{:S(2)}) copy-start(f32[256,1024]{1,0:T(8,128)} %get-tuple-element.61) | copy-start | bytes 3145732
  141.2 1.0 copy-start.7
  141.2 1.6 %copy-start.4 = (f32[256,256]{1,0:T(8,128)S(1)}, f32[256,256]{1,0:T(8,128)}, u32[]{:S(2)}) copy-start(f32[256,256]{1,0:T(8,128)} %get-tuple-element.64) | copy-start | bytes 786436
  141.2 2.3 %copy-start.1 = (f32[256,1024]{1,0:T(8,128)S(1)}, f32[256,1024]{1,0:T(8,128)}, u32[]{:S(2)}) copy-start(f32[256,1024]{1,0:T(8,128)} %get-tuple-element.65) | copy-start | bytes 3145732
  143.4 1.0 copy-start.6
  143.4 1.6 %copy-start = (f32[256,1024]{1,0:T(8,128)S(1)}, f32[256,1024]{1,0:T(8,128)}, u32[]{:S(2)}) copy-start(f32[256,1024]{1,0:T(8,128)} %get-tuple-element.67) | copy-start | bytes 3145732
  145.0 1.0 copy-start.8
  146.0 0.7 copy-start.5
